TPU v7x, 32 devices: a whole 2x2x4 slice. The times are simulated.
32 devices in a mesh: gx: 16 (over z, y, core), gz: 2 (over x).
Axes of the slice: x: 2, y: 2, z: 4, core: 2. Of those that a mesh axis runs over, the one named last changes fastest.
Arguments:
- strain_inc: float32 [6, 32, 256, 256], P(None, 'gx', None, 'gz'), may hold values from -2.5 to 2.5
- stress_old: float32 [6, 32, 256, 256], P(None, 'gx', None, 'gz'), may hold values from -6 to 6
- material_id: int32 [32, 256, 256], P('gx', None, 'gz'), may hold values from 0 to 7
- cohesion: float32 [8], replicated, may hold values from 1 to 4
- friction: float32 [8], replicated, may hold values from 0.05 to 0.3
- pressure: float32 [32, 256, 256], P('gx', 'gz'), may hold values from -6 to 6
- storage: float32 [32, 256, 256], P('gx', 'gz'), may hold values from 0.5 to 4
- perm_class: int32 [32, 256, 256], P('gx', 'gz'), may hold values from 0 to 15
- perm_table: float32 [16], replicated, may hold values from 0.5 to 8
Outputs:
- pressure_next: float32 [32, 256, 256], P('gx', 'gz')
- stress_next: float32 [6, 32, 256, 256], P(None, 'gx', None, 'gz')
- node_force: float32 [3, 32, 256, 256], P(None, 'gx', None, 'gz')
All inputs are finite; a program needn't handle non-finite values.
Results may differ from a plain program's by a relative error of at most 0.00002.
Values sent between devices are 32-bit elements; how exact they have to be, the bound alone decides.
A program may use at most 64 MiB of HBM per device.

v0:
```python
import jax
import jax.numpy as jnp
from jax import lax
from jax.sharding import PartitionSpec as P

BIOT = 0.8
SHEAR = 1.0
BULK = 1.5
FLOOR = 0.25
TINY = 1e-30


def extended(array, sides, width):
    for axis, dim in sides:
        count, length = (lax.axis_size(axis), array.shape[dim])
        up = [(i, (i + 1) % count) for i in range(count - 1)]
        down = [(j, i) for i, j in up]
        last = lax.slice_in_dim(array, length - width, length, axis=dim)
        leading = lax.slice_in_dim(array, 0, width, axis=dim)
        before = lax.ppermute(last, axis, up)
        after = lax.ppermute(leading, axis, down)
        array = jnp.concatenate([before, array, after], axis=dim)
    return array


def passed_along(block, axis, distance):
    devices = range(lax.axis_size(axis))
    route = [(i - distance, i) for i in devices if i - distance in devices]
    return lax.ppermute(block, axis, route)


def lookup(ids, table):
    result = jnp.zeros(ids.shape, jnp.float32)
    for entry in range(table.shape[0]):
        result = result + jnp.where(ids == entry, table[entry], jnp.zeros((), jnp.float32))
    return result


def neighbours():
    inner = slice(1, -1)
    return [
        (slice(2, None), inner, inner),
        (slice(0, -2), inner, inner),
        (inner, slice(2, None), inner),
        (inner, slice(0, -2), inner),
        (inner, inner, slice(2, None)),
        (inner, inner, slice(0, -2)),
    ]


def relax_padded(pressure_pad, cond_pad, storage, source):
    conduct = cond_pad[1:-1, 1:-1, 1:-1]
    numerator = source
    denominator = storage
    for offset in neighbours():
        cond_near = cond_pad[offset]
        transmit = 2.0 * conduct * cond_near / jnp.maximum(conduct + cond_near, TINY)
        numerator = numerator + transmit * pressure_pad[offset]
        denominator = denominator + transmit
    denominator = jnp.where(denominator > 0.0, denominator, jnp.ones((), jnp.float32))
    return numerator / denominator


def plastic(strain_inc, stress_old, material_id, cohesion, friction):
    normal_mask = jnp.array([1.0, 1.0, 1.0, 0.0, 0.0, 0.0], jnp.float32).reshape(6, 1, 1, 1)
    volume = strain_inc[0] + strain_inc[1] + strain_inc[2]
    trial_stress = (
        stress_old
        + 2.0 * SHEAR * (strain_inc - normal_mask * (volume / 3.0))
        + BULK * volume * normal_mask
    )
    first_invariant = trial_stress[0] + trial_stress[1] + trial_stress[2]
    deviator = trial_stress - normal_mask * (first_invariant / 3.0)
    second_invariant = 0.5 * (
        deviator[0] * deviator[0] + deviator[1] * deviator[1] + deviator[2] * deviator[2]
    )
    second_invariant = (
        second_invariant
        + deviator[3] * deviator[3]
        + deviator[4] * deviator[4]
        + deviator[5] * deviator[5]
    )
    equiv_shear = jnp.sqrt(second_invariant)
    strength = lookup(material_id, cohesion)
    slope = lookup(material_id, friction)
    yield_value = equiv_shear + slope * first_invariant - strength
    multiplier = jnp.maximum(yield_value, 0.0) / (SHEAR + 9.0 * BULK * slope * slope)
    shrink_factor = jnp.maximum(1.0 - SHEAR * multiplier / jnp.maximum(equiv_shear, FLOOR), 0.0)
    new_invariant = first_invariant - 9.0 * BULK * slope * multiplier
    return deviator * shrink_factor + normal_mask * (new_invariant / 3.0)


def corner_terms(stress_next, pressure_block):
    normal_mask = jnp.array([1.0, 1.0, 1.0, 0.0, 0.0, 0.0], jnp.float32).reshape(6, 1, 1, 1)
    total = stress_next - BIOT * pressure_block * normal_mask
    col_x = jnp.stack([total[0], total[3], total[5]])
    col_y = jnp.stack([total[3], total[1], total[4]])
    col_z = jnp.stack([total[5], total[4], total[2]])
    return (col_x, col_y, col_z)


def place_corner(term, along_x, along_y):
    placed = jnp.pad(term, ((0, 0), (along_x, 1 - along_x), (0, 0), (0, 0)))
    if along_y == 1:
        placed = jnp.pad(placed, ((0, 0), (0, 0), (1, 0), (0, 0)))[:, :, :-1]
    return placed


def node_parts(col_x, col_y, col_z):
    lower = None
    upper = None
    for corner in range(8):
        along_x = corner & 1
        along_y = corner >> 1 & 1
        along_z = corner >> 2
        term = 0.25 * (
            (2 * along_x - 1) * col_x + (2 * along_y - 1) * col_y + (2 * along_z - 1) * col_z
        )
        placed = place_corner(term, along_x, along_y)
        if along_z == 0:
            lower = placed if lower is None else lower + placed
        else:
            upper = placed if upper is None else upper + placed
    node_main = lower + jnp.pad(upper[..., :-1], ((0, 0), (0, 0), (0, 0), (1, 0)))
    node_rim = upper[..., -1]
    return (node_main, node_rim)


def on_device(
    strain_inc,
    stress_old,
    material_id,
    cohesion,
    friction,
    pressure,
    storage,
    perm_class,
    perm_table,
):
    strain_rate = strain_inc[0] + strain_inc[1] + strain_inc[2]
    rate_column = lax.all_to_all(strain_rate, "gz", split_axis=1, concat_axis=2, tiled=True)
    stress_next = plastic(strain_inc, stress_old, material_id, cohesion, friction)
    conduct = lookup(perm_class, perm_table)
    source = storage * pressure - BIOT * rate_column
    pressure_pair = extended(jnp.stack([pressure, conduct]), (("gx", 1), ("gz", 2)), 1)
    pressure_pair = jnp.pad(pressure_pair, ((0, 0), (0, 0), (0, 0), (1, 1)))
    first_sweep = relax_padded(pressure_pair[0], pressure_pair[1], storage, source)
    bordered = extended(first_sweep, (("gx", 0), ("gz", 1)), 1)
    bordered = jnp.pad(bordered, ((0, 0), (0, 0), (1, 1)))
    pressure_next = relax_padded(bordered, pressure_pair[1], storage, source)
    pressure_block = lax.all_to_all(pressure_next, "gz", split_axis=2, concat_axis=1, tiled=True)
    col_x, col_y, col_z = corner_terms(stress_next, pressure_block)
    node_main, node_rim = node_parts(col_x, col_y, col_z)
    from_below = passed_along(node_rim, "gz", 1)
    node_main = node_main.at[:, :, :, 0].add(from_below)
    slab_plane = passed_along(node_main[:, -1], "gx", 1)
    node_main = node_main.at[:, 0].add(slab_plane)
    node_force = node_main[:, :-1]
    return (pressure_next, stress_next, node_force)


def solution(mesh):
    in_specs = (
        P(None, "gx", None, "gz"),
        P(None, "gx", None, "gz"),
        P("gx", None, "gz"),
        P(),
        P(),
        P("gx", "gz", None),
        P("gx", "gz", None),
        P("gx", "gz", None),
        P(),
    )
    out_specs = (P("gx", "gz", None), P(None, "gx", None, "gz"), P(None, "gx", None, "gz"))
    return jax.shard_map(
        on_device, mesh=mesh, in_specs=in_specs, out_specs=out_specs, check_vma=False
    )
```

profile of v0, /device:TPU:10, one launch (start us, length us, event | category | flops | bytes accessed | tf_op | source)
XLA Modules:
  0.0 118.8 jit_solution(4340846625910367335)
XLA Ops:
  0.6 1.9 %fusion.46 = (f32[1]{0:T(128)}, f32[1]{0:T(128)}, f32[1]{0:T(128)}, f32[1]{0:T(128)}, f32[1]{0:T(128)}, /*index=5*/f32[1]{0:T(128)}, f32[1]{0:T(128)}, f32[1]{0:...) fusion(f32[16]{0:T(128)} %param.23), kind=kLoop, calls=%fused_computation.149 | loop fusion | bytes 128 | tf_op jit(solution)/shard_map/slice | solution.py:35
  2.6 12.0 %add_bitcast_fusion = f32[1,2,128,256]{3,2,1,0:T(8,128)} fusion(s32[2,128,256]{2,1,0:T(8,128)} %param.22, f32[]{:T(128)} %bitcast.19, f32[]{:T(128)} %bitcast.18, f32[]{:T(128)} %bitcast.17, f32[]{:T(128)} %bitcast.16, f32[]{:T(128)} %bitcast.15, f32[]{:T(128)} %bitcast.14, f32[]{:T(128)} %bitcast.13, f32[]{:T(128)} %bitcast.12, f32[]{:T(128)} %bitcast.11, ...), kind=kLoop, calls=%fused_computation.125 | loop fusion | flops 3080192 | bytes 524352 | tf_op jit(solution)/shard_map/stack | solution.py:145
  14.6 1.9 %fusion.11 = (f32[2,1,128,256]{3,2,1,0:T(8,128)}, f32[2,1,128,256]{3,2,1,0:T(8,128)}) fusion(f32[1,2,128,256]{3,2,1,0:T(8,128)} %bitcast.79, f32[1,2,128,256]{3,2,1,0:T(8,128)} %add_bitcast_fusion), kind=kLoop, calls=%fused_computation.57 | loop fusion | flops 131072 | bytes 1048576 | tf_op jit(solution)/shard_map/stack | solution.py:145
  16.5 2.0 %collective-permute-start = (f32[2,1,128,256]{3,2,1,0:T(8,128)}, f32[2,1,128,256]{3,2,1,0:T(8,128)}, u32[]{:S(2)}, u32[]{:S(2)}) collective-permute-start(f32[2,1,128,256]{3,2,1,0:T(8,128)} %get-tuple-element.84), channel_id=1, source_target_pairs={{0,2},{2,4},{4,6},{6,8},{8,10},{10,12},{12,14},{14,16},{16,18},{18... | collective-permute-start | bytes 786440 | tf_op jit(solution)/shard_map/ppermute | solution.py:20
  18.6 4.5 %collective-permute-start.1 = (f32[2,1,128,256]{3,2,1,0:T(8,128)}, f32[2,1,128,256]{3,2,1,0:T(8,128)}, u32[]{:S(2)}, u32[]{:S(2)}) collective-permute-start(f32[2,1,128,256]{3,2,1,0:T(8,128)} %get-tuple-element.85), channel_id=1, source_target_pairs={{2,0},{4,2},{6,4},{8,6},{10,8},{12,10},{14,12},{16,14},{18,16},{20... | collective-permute-start | bytes 786440 | tf_op jit(solution)/shard_map/ppermute | solution.py:21
  23.2 0.9 copy.250
  24.1 4.6 %all-to-all-start = ((f32[2,256,128]{2,0,1:T(2,128)}), f32[2,256,128]{2,0,1:T(2,128)}, u32[]{:S(2)}, u32[]{:S(2)}) async-start(f32[2,256,128]{2,0,1:T(2,128)} %copy.250), calls=%async_computation | async-start | bytes 524288 | tf_op jit(solution)/shard_map/all_to_all | solution.py:141
  28.8 1.8 %multiply_add_fusion.1 = f32[6,2,256,128]{3,2,1,0:T(8,128)S(1)} fusion(f32[6,2,256,128]{3,2,1,0:T(8,128)} %param.16, f32[6,2,256,128]{3,2,1,0:T(8,128)S(1)} %copy-done.1, f32[2,256,128]{2,1,0:T(8,128)S(1)} %multiply_bitcast_fusion.1, f32[2,256,128]{2,1,0:T(8,128)S(1)} %get-tuple-element.62, f32[6]{0:T(128)S(1)} %copy-done.18), kind=kLoop, calls=%fused_computation.11 | loop fusion | flops 2359296 | bytes 5242904 | tf_op jit(solution)/shard_map/add | solution.py:68
  30.5 0.8 multiply_bitcast_fusion
  31.3 0.2 multiply_subtract_fusion.1
  31.6 0.5 copy-done.2
  32.0 0.3 copy-done
  32.4 0.8 pad_maximum_fusion.15
  33.2 1.3 %collective-permute-start.2 = (f32[2,4,1,256]{3,1,2,0:T(4,128)S(1)}, f32[2,4,1,256]{3,1,2,0:T(4,128)S(1)}, u32[]{:S(2)}, u32[]{:S(2)}) collective-permute-start(f32[2,4,1,256]{3,1,2,0:T(4,128)S(1)} %copy.252), channel_id=1, source_target_pairs={{0,1},{2,3},{4,5},{6,7},{8,9},{10,11},{12,13},{14,15},{16,17},{18,... | collective-permute-start | bytes 24584 | tf_op jit(solution)/shard_map/ppermute | solution.py:20
  34.5 4.5 %collective-permute-start.3 = (f32[2,4,1,256]{3,1,2,0:T(4,128)S(1)}, f32[2,4,1,256]{3,1,2,0:T(4,128)S(1)}, u32[]{:S(2)}, u32[]{:S(2)}) collective-permute-start(f32[2,4,1,256]{3,1,2,0:T(4,128)S(1)} %copy.253), channel_id=1, source_target_pairs={{1,0},{3,2},{5,4},{7,6},{9,8},{11,10},{13,12},{15,14},{17,16},{19,... | collective-permute-start | bytes 24584 | tf_op jit(solution)/shard_map/ppermute | solution.py:21
  39.1 1.1 broadcast_multiply_fusion.1
  40.2 0.9 copy.261
  41.1 1.9 %mul.296 = f32[2,128,256]{2,1,0:T(8,128)} reshape(f32[2,128,2,128]{3,2,1,0:T(2,128)} %bitcast.85) | data formatting | bytes 524288 | tf_op jit(solution)/shard_map/mul | solution.py:144
  43.0 1.7 %select_maximum_fusion = f32[2,4,130,258]{3,2,1,0:T(8,128)S(1)} fusion(f32[2,4,1,256]{3,2,1,0:T(1,128)S(1)} %copy.255, f32[2,4,1,256]{3,2,1,0:T(1,128)S(1)} %copy.254, f32[2,1,128,256]{3,2,1,0:T(8,128)} %collective-permute-done.1, f32[2,1,128,256]{3,2,1,0:T(8,128)} %collective-permute-done, f32[1,2,128,256]{3,2,1,0:T(8,128)} %add_bitcast_fusion, ...), kind=kLoop, calls=%fused_computation.2 | loop fusion | flops 3756480 | bytes 2138240 | tf_op jit(solution)/shard_map/concatenate | solution.py:22
  44.8 0.8 copy-done.6
  45.7 0.9 fusion.32
  46.7 1.9 %collective-permute-start.4 = (f32[1,128,256]{2,1,0:T(8,128)S(1)}, f32[1,128,256]{2,1,0:T(8,128)S(1)}, u32[]{:S(2)}, u32[]{:S(2)}) collective-permute-start(f32[1,128,256]{2,1,0:T(8,128)S(1)} %get-tuple-element.87), channel_id=1, source_target_pairs={{2,0},{4,2},{6,4},{8,6},{10,8},{12,10},{14,12},{16,14},{18,16},{20... | collective-permute-start | bytes 393224 | tf_op jit(solution)/shard_map/ppermute | solution.py:21
  48.6 2.4 %collective-permute-start.5 = (f32[1,128,256]{2,1,0:T(8,128)S(1)}, f32[1,128,256]{2,1,0:T(8,128)S(1)}, u32[]{:S(2)}, u32[]{:S(2)}) collective-permute-start(f32[1,128,256]{2,1,0:T(8,128)S(1)} %get-tuple-element.86), channel_id=1, source_target_pairs={{0,2},{2,4},{4,6},{6,8},{8,10},{10,12},{12,14},{14,16},{16,18},{18... | collective-permute-start | bytes 393224 | tf_op jit(solution)/shard_map/ppermute | solution.py:20
  51.0 0.7 fusion.44
  51.7 0.7 fusion.45
  52.4 3.4 %collective-permute-done.5 = f32[1,128,256]{2,1,0:T(8,128)S(1)} collective-permute-done((f32[1,128,256]{2,1,0:T(8,128)S(1)}, f32[1,128,256]{2,1,0:T(8,128)S(1)}, u32[]{:S(2)}, u32[]{:S(2)}) %collective-permute-start.5) | collective-permute-done | bytes 131104 | tf_op jit(solution)/shard_map/ppermute | solution.py:20
  55.8 1.6 %collective-permute-start.6 = (f32[4,1,256]{2,1,0:T(1,128)S(1)}, f32[4,1,256]{2,1,0:T(1,128)S(1)}, u32[]{:S(2)}, u32[]{:S(2)}) collective-permute-start(f32[4,1,256]{2,1,0:T(1,128)S(1)} %get-tuple-element.83), channel_id=1, source_target_pairs={{1,0},{3,2},{5,4},{7,6},{9,8},{11,10},{13,12},{15,14},{17,16},{19,... | collective-permute-start | bytes 12296 | tf_op jit(solution)/shard_map/ppermute | solution.py:21
  57.4 1.3 %collective-permute-start.7 = (f32[4,1,256]{2,1,0:T(1,128)S(1)}, f32[4,1,256]{2,1,0:T(1,128)S(1)}, u32[]{:S(2)}, u32[]{:S(2)}) collective-permute-start(f32[4,1,256]{2,1,0:T(1,128)S(1)} %get-tuple-element.82), channel_id=1, source_target_pairs={{0,1},{2,3},{4,5},{6,7},{8,9},{10,11},{12,13},{14,15},{16,17},{18,... | collective-permute-start | bytes 12296 | tf_op jit(solution)/shard_map/ppermute | solution.py:20
  58.8 11.5 %subtract_maximum_fusion = (f32[2,256,128]{2,1,0:T(8,128)}, f32[2,256,128]{2,1,0:T(8,128)}, pred[2,256,128]{2,1,0:T(8,128)(4,1)S(1)}, pred[2,256,128]{2,1,0:T(8,...) fusion(f32[]{:T(128)} %bitcast.43, f32[]{:T(128)} %bitcast.42, ...), kind=kLoop, calls=%fused_computation.114 | loop fusion | flops 4063232 | bytes 3145792 | tf_op jit(solution)/shard_map/max | solution.py:88
  70.3 0.3 select_maximum_fusion.5
  70.7 0.8 fusion.21
  71.5 0.7 copy-done.10
  72.2 0.8 copy.256
  73.0 6.2 %all-to-all-start.1 = ((f32[2,128,256]{1,0,2:T(2,128)}), f32[2,128,256]{1,0,2:T(2,128)S(1)}, u32[]{:S(2)}, u32[]{:S(2)}) async-start(f32[2,128,256]{1,0,2:T(2,128)} %copy.256), calls=%async_computation.1 | async-start | bytes 524288 | tf_op jit(solution)/shard_map/all_to_all | solution.py:151
  79.2 11.2 %fusion.10 = f32[2,256,128]{2,1,0:T(8,128)S(1)} fusion(f32[1,2,256,128]{3,2,1,0:T(8,128)S(1)} %copy-done.5, pred[2,256,128]{2,1,0:T(8,128)(4,1)} %get-tuple-element.59, f32[]{:T(128)} %bitcast.43, pred[2,256,128]{2,1,0:T(8,128)(4,1)} %get-tuple-element.58, f32[]{:T(128)} %bitcast.42, pred[2,256,128]{2,1,0:T(8,128)(4,1)S(1)} %copy-done.15, f32[]{:T(128)} %bitcast.41, ...), kind=kLoop, calls=%fused_computation.56 | loop fusion | flops 2686976 | bytes 1310784 | tf_op jit(solution)/shard_map/div | solution.py:90
  90.8 1.6 %multiply_subtract_fusion = (f32[6,2,256,128]{3,2,1,0:T(8,128)S(1)}, f32[6,2,256,128]{3,2,1,0:T(8,128)}) fusion(f32[2,256,128]{2,1,0:T(8,128)S(1)} %bitcast.83, f32[6]{0:T(128)S(1)} %copy-done.18, f32[2,256,128]{2,1,0:T(8,128)S(1)} %fusion.10, f32[2,256,128]{2,1,0:T(8,128)S(1)} %copy-done.7, f32[6,2,256,128]{3,2,1,0:T(8,128)S(1)} %multiply_add_fusion.1, ...), kind=kLoop, calls=%fused_computation.8 | loop fusion | flops 2752512 | bytes 5767192 | tf_op jit(solution)/shard_map/sub | solution.py:95
  92.5 0.2 add_multiply_fusion.7
  92.8 0.2 add_multiply_fusion
  93.0 0.2 add_multiply_fusion.4
  93.4 0.7 slice_reduce_fusion
  94.2 1.3 %collective-permute-start.8 = (f32[3,3,256]{2,1,0:T(4,128)S(1)}, f32[3,3,256]{2,1,0:T(4,128)S(1)}, u32[]{:S(2)}, u32[]{:S(2)}) collective-permute-start(f32[3,3,256]{2,1,0:T(4,128)S(1)} %slice_reduce_fusion), channel_id=1, source_target_pairs={{0,1},{2,3},{4,5},{6,7},{8,9},{10,11},{12,13},{14,15},{16,17},{18,... | collective-permute-start | bytes 27656 | tf_op jit(solution)/shard_map/ppermute | solution.py:29
  95.5 0.5 fusion.3
  96.0 3.8 %collective-permute-done.8 = f32[3,3,256]{2,1,0:T(4,128)S(1)} collective-permute-done((f32[3,3,256]{2,1,0:T(4,128)S(1)}, f32[3,3,256]{2,1,0:T(4,128)S(1)}, u32[]{:S(2)}, u32[]{:S(2)}) %collective-permute-start.8) | collective-permute-done | bytes 9248 | tf_op jit(solution)/shard_map/ppermute | solution.py:29
  99.7 0.4 copy.258
  100.3 7.5 %scatter-add.6 = f32[3,3,256,128]{3,2,1,0:T(8,128)S(1)} dynamic-update-slice(f32[3,3,256,128]{3,2,1,0:T(8,128)S(1)} %fusion.3, f32[3,3,256,1]{3,2,1,0:T(8,128)S(1)} %slice_add_fusion, s32[]{:T(128)} %constant.100.clone.1, s32[]{:T(128)} %constant.100.clone.1, s32[]{:T(128)} %constant.100.clone.1, s32[]{:T(128)} %constant.100.clone.1) | dynamic-update-slice | bytes 18436 | tf_op jit(solution)/shard_map/scatter-add | solution.py:155
  107.8 1.9 %collective-permute-start.9 = (f32[3,256,128]{2,1,0:T(8,128)S(1)}, f32[3,256,128]{2,1,0:T(8,128)S(1)}, u32[]{:S(2)}, u32[]{:S(2)}) collective-permute-start(f32[3,256,128]{2,1,0:T(8,128)S(1)} %slice_bitcast_fusion.2), channel_id=1, source_target_pairs={{0,2},{2,4},{4,6},{6,8},{8,10},{10,12},{12,14},{14,16},{16,18},{18... | collective-permute-start | bytes 1179656 | tf_op jit(solution)/shard_map/ppermute | solution.py:29
  109.7 8.1 %collective-permute-done.9 = f32[3,256,128]{2,1,0:T(8,128)S(1)} collective-permute-done((f32[3,256,128]{2,1,0:T(8,128)S(1)}, f32[3,256,128]{2,1,0:T(8,128)S(1)}, u32[]{:S(2)}, u32[]{:S(2)}) %collective-permute-start.9) | collective-permute-done | bytes 393248 | tf_op jit(solution)/shard_map/ppermute | solution.py:29
  117.9 0.9 slice.475
  (60 shorter events, 1.4 us)
Async XLA Ops:
  0.6 22.5 %copy-start.1 = (f32[6,2,256,128]{3,2,1,0:T(8,128)S(1)}, f32[6,2,256,128]{3,2,1,0:T(8,128)}, u32[]{:S(2)}) copy-start(f32[6,2,256,128]{3,2,1,0:T(8,128)} %param.15) | copy-start | bytes 4718596
  16.5 12.2 %copy-start.18 = (f32[6]{0:T(128)S(1)}, f32[6]{0:T(128)}, u32[]{:S(2)}) copy-start(f32[6]{0:T(128)} %constant.126.clone) | copy-start | bytes 76
  16.5 15.5 %collective-permute-start = (f32[2,1,128,256]{3,2,1,0:T(8,128)}, f32[2,1,128,256]{3,2,1,0:T(8,128)}, u32[]{:S(2)}, u32[]{:S(2)}) collective-permute-start(f32[2,1,128,256]{3,2,1,0:T(8,128)} %get-tuple-element.84), channel_id=1, source_target_pairs={{0,2},{2,4},{4,6},{6,8},{8,10},{10,12},{12,14},{14,16},{16,18},{18... | collective-permute-start | bytes 786440 | tf_op jit(solution)/shard_map/ppermute | solution.py:20
  18.6 13.5 %collective-permute-start.1 = (f32[2,1,128,256]{3,2,1,0:T(8,128)}, f32[2,1,128,256]{3,2,1,0:T(8,128)}, u32[]{:S(2)}, u32[]{:S(2)}) collective-permute-start(f32[2,1,128,256]{3,2,1,0:T(8,128)} %get-tuple-element.85), channel_id=1, source_target_pairs={{2,0},{4,2},{6,4},{8,6},{10,8},{12,10},{14,12},{16,14},{18,16},{20... | collective-permute-start | bytes 786440 | tf_op jit(solution)/shard_map/ppermute | solution.py:21
  24.1 14.9 %all-to-all-start = ((f32[2,256,128]{2,0,1:T(2,128)}), f32[2,256,128]{2,0,1:T(2,128)}, u32[]{:S(2)}, u32[]{:S(2)}) async-start(f32[2,256,128]{2,0,1:T(2,128)} %copy.250), calls=%async_computation | async-start | bytes 524288 | tf_op jit(solution)/shard_map/all_to_all | solution.py:141
  31.3 0.7 copy-start.2
  31.3 1.0 copy-start
  33.2 9.7 %collective-permute-start.2 = (f32[2,4,1,256]{3,1,2,0:T(4,128)S(1)}, f32[2,4,1,256]{3,1,2,0:T(4,128)S(1)}, u32[]{:S(2)}, u32[]{:S(2)}) collective-permute-start(f32[2,4,1,256]{3,1,2,0:T(4,128)S(1)} %copy.252), channel_id=1, source_target_pairs={{0,1},{2,3},{4,5},{6,7},{8,9},{10,11},{12,13},{14,15},{16,17},{18,... | collective-permute-start | bytes 24584 | tf_op jit(solution)/shard_map/ppermute | solution.py:20
  34.5 8.4 %collective-permute-start.3 = (f32[2,4,1,256]{3,1,2,0:T(4,128)S(1)}, f32[2,4,1,256]{3,1,2,0:T(4,128)S(1)}, u32[]{:S(2)}, u32[]{:S(2)}) collective-permute-start(f32[2,4,1,256]{3,1,2,0:T(4,128)S(1)} %copy.253), channel_id=1, source_target_pairs={{1,0},{3,2},{5,4},{7,6},{9,8},{11,10},{13,12},{15,14},{17,16},{19,... | collective-permute-start | bytes 24584 | tf_op jit(solution)/shard_map/ppermute | solution.py:21
  44.7 1.0 copy-start.6
  44.7 1.0 copy-start.9
  45.7 5.3 %copy-start.16 = (f32[8]{0:T(128)S(1)}, f32[8]{0:T(128)}, u32[]{:S(2)}) copy-start(f32[8]{0:T(128)} %param.19) | copy-start | bytes 100
  45.7 6.0 %copy-start.17 = (f32[8]{0:T(128)S(1)}, f32[8]{0:T(128)}, u32[]{:S(2)}) copy-start(f32[8]{0:T(128)} %param.18) | copy-start | bytes 100
  45.7 13.0 %copy-start.4 = (f32[1,2,256,128]{3,2,1,0:T(8,128)S(1)}, f32[1,2,256,128]{3,2,1,0:T(8,128)}, u32[]{:S(2)}) copy-start(f32[1,2,256,128]{3,2,1,0:T(8,128)} %get-tuple-element.61) | copy-start | bytes 786436
  45.7 13.0 %copy-start.11 = (s32[2,256,128]{2,1,0:T(8,128)S(1)}, s32[2,256,128]{2,1,0:T(8,128)}, u32[]{:S(2)}) copy-start(s32[2,256,128]{2,1,0:T(8,128)} %param.17) | copy-start | bytes 786436
  46.7 5.7 %collective-permute-start.4 = (f32[1,128,256]{2,1,0:T(8,128)S(1)}, f32[1,128,256]{2,1,0:T(8,128)S(1)}, u32[]{:S(2)}, u32[]{:S(2)}) collective-permute-start(f32[1,128,256]{2,1,0:T(8,128)S(1)} %get-tuple-element.87), channel_id=1, source_target_pairs={{2,0},{4,2},{6,4},{8,6},{10,8},{12,10},{14,12},{16,14},{18,16},{20... | collective-permute-start | bytes 393224 | tf_op jit(solution)/shard_map/ppermute | solution.py:21
  48.6 7.2 %collective-permute-start.5 = (f32[1,128,256]{2,1,0:T(8,128)S(1)}, f32[1,128,256]{2,1,0:T(8,128)S(1)}, u32[]{:S(2)}, u32[]{:S(2)}) collective-permute-start(f32[1,128,256]{2,1,0:T(8,128)S(1)} %get-tuple-element.86), channel_id=1, source_target_pairs={{0,2},{2,4},{4,6},{6,8},{8,10},{10,12},{12,14},{14,16},{16,18},{18... | collective-permute-start | bytes 393224 | tf_op jit(solution)/shard_map/ppermute | solution.py:20
  55.8 14.5 %collective-permute-start.6 = (f32[4,1,256]{2,1,0:T(1,128)S(1)}, f32[4,1,256]{2,1,0:T(1,128)S(1)}, u32[]{:S(2)}, u32[]{:S(2)}) collective-permute-start(f32[4,1,256]{2,1,0:T(1,128)S(1)} %get-tuple-element.83), channel_id=1, source_target_pairs={{1,0},{3,2},{5,4},{7,6},{9,8},{11,10},{13,12},{15,14},{17,16},{19,... | collective-permute-start | bytes 12296 | tf_op jit(solution)/shard_map/ppermute | solution.py:21
  57.4 12.8 %collective-permute-start.7 = (f32[4,1,256]{2,1,0:T(1,128)S(1)}, f32[4,1,256]{2,1,0:T(1,128)S(1)}, u32[]{:S(2)}, u32[]{:S(2)}) collective-permute-start(f32[4,1,256]{2,1,0:T(1,128)S(1)} %get-tuple-element.82), channel_id=1, source_target_pairs={{0,1},{2,3},{4,5},{6,7},{8,9},{10,11},{12,13},{14,15},{16,17},{18,... | collective-permute-start | bytes 12296 | tf_op jit(solution)/shard_map/ppermute | solution.py:20
  70.6 8.6 %copy-start.5 = (f32[1,2,256,128]{3,2,1,0:T(8,128)S(1)}, f32[1,2,256,128]{3,2,1,0:T(8,128)}, u32[]{:S(2)}) copy-start(f32[1,2,256,128]{3,2,1,0:T(8,128)} %get-tuple-element.61) | copy-start | bytes 786436
  70.6 8.6 %copy-start.8 = (f32[2,256,128]{2,1,0:T(8,128)S(1)}, f32[2,256,128]{2,1,0:T(8,128)}, u32[]{:S(2)}) copy-start(f32[2,256,128]{2,1,0:T(8,128)} %get-tuple-element.51) | copy-start | bytes 786436
  70.6 8.6 %copy-start.12 = (pred[2,256,128]{2,1,0:T(8,128)(4,1)S(1)}, pred[2,256,128]{2,1,0:T(8,128)(4,1)}, u32[]{:S(2)}) copy-start(pred[2,256,128]{2,1,0:T(8,128)(4,1)} %get-tuple-element.54) | copy-start | bytes 196612
  70.6 8.6 %copy-start.13 = (pred[2,256,128]{2,1,0:T(8,128)(4,1)S(1)}, pred[2,256,128]{2,1,0:T(8,128)(4,1)}, u32[]{:S(2)}) copy-start(pred[2,256,128]{2,1,0:T(8,128)(4,1)} %get-tuple-element.55) | copy-start | bytes 196612
  70.6 8.6 %copy-start.14 = (pred[2,256,128]{2,1,0:T(8,128)(4,1)S(1)}, pred[2,256,128]{2,1,0:T(8,128)(4,1)}, u32[]{:S(2)}) copy-start(pred[2,256,128]{2,1,0:T(8,128)(4,1)} %get-tuple-element.56) | copy-start | bytes 196612
  70.7 8.6 %copy-start.15 = (pred[2,256,128]{2,1,0:T(8,128)(4,1)S(1)}, pred[2,256,128]{2,1,0:T(8,128)(4,1)}, u32[]{:S(2)}) copy-start(pred[2,256,128]{2,1,0:T(8,128)(4,1)} %get-tuple-element.57) | copy-start | bytes 196612
  71.5 0.7 copy-start.10
  73.0 17.7 %copy-start.3 = (f32[2,256,128]{2,1,0:T(8,128)S(1)}, f32[2,256,128]{2,1,0:T(8,128)}, u32[]{:S(2)}) copy-start(f32[2,256,128]{2,1,0:T(8,128)} %copy-done.2) | copy-start | bytes 786436
  73.0 17.7 %copy-start.7 = (f32[2,256,128]{2,1,0:T(8,128)S(1)}, f32[2,256,128]{2,1,0:T(8,128)}, u32[]{:S(2)}) copy-start(f32[2,256,128]{2,1,0:T(8,128)} %get-tuple-element.50) | copy-start | bytes 786436
  73.0 17.4 %all-to-all-start.1 = ((f32[2,128,256]{1,0,2:T(2,128)}), f32[2,128,256]{1,0,2:T(2,128)S(1)}, u32[]{:S(2)}, u32[]{:S(2)}) async-start(f32[2,128,256]{1,0,2:T(2,128)} %copy.256), calls=%async_computation.1 | async-start | bytes 524288 | tf_op jit(solution)/shard_map/all_to_all | solution.py:151
  94.2 5.6 %collective-permute-start.8 = (f32[3,3,256]{2,1,0:T(4,128)S(1)}, f32[3,3,256]{2,1,0:T(4,128)S(1)}, u32[]{:S(2)}, u32[]{:S(2)}) collective-permute-start(f32[3,3,256]{2,1,0:T(4,128)S(1)} %slice_reduce_fusion), channel_id=1, source_target_pairs={{0,1},{2,3},{4,5},{6,7},{8,9},{10,11},{12,13},{14,15},{16,17},{18,... | collective-permute-start | bytes 27656 | tf_op jit(solution)/shard_map/ppermute | solution.py:29
  107.8 10.0 %collective-permute-start.9 = (f32[3,256,128]{2,1,0:T(8,128)S(1)}, f32[3,256,128]{2,1,0:T(8,128)S(1)}, u32[]{:S(2)}, u32[]{:S(2)}) collective-permute-start(f32[3,256,128]{2,1,0:T(8,128)S(1)} %slice_bitcast_fusion.2), channel_id=1, source_target_pairs={{0,2},{2,4},{4,6},{6,8},{8,10},{10,12},{12,14},{14,16},{16,18},{18... | collective-permute-start | bytes 1179656 | tf_op jit(solution)/shard_map/ppermute | solution.py:29
where the time goes:
time: 120 us; the launch traced here: 119 us
  other arithmetic  48.5 us (40%)
  starting transfers between devices  33.7 us (28%)
  local copies, waits for them, and re-layouts  20.2 us (17%)
  waiting for transfers between devices  15.3 us (13%)
    another operation x2, other arithmetic, on_device(): jnp.stack([pressure, conduct])  13.9 us
    ppermute x4, starting transfers between devices, extended(): after = lax.ppermute(leading, axis, down)  12.6 us
    ppermute x2, waiting for transfers between devices, passed_along(): return lax.ppermute(block, axis, route)  11.9 us
    max x1, other arithmetic, plastic(): jnp.maximum(1.0 - SHEAR * multiplier / jnp.maximum(equiv_shear, FLOOR), 0.0)  11.5 us
    div x1, other arithmetic, plastic(): return deviator * shrink_factor + normal_mask * (new_invariant / 3.0)  11.2 us
    scatter-add x1, local copies, waits for them, and re-layouts, on_device(): node_main = node_main.at[:, :, :, 0].add(from_below)  7.48 us
    ppermute x4, starting transfers between devices, extended(): before = lax.ppermute(last, axis, up)  7.03 us
    all_to_all x1, starting transfers between devices, on_device(): lax.all_to_all(pressure_next, 'gz', split_axis=2, concat_axis=1, tiled=True)  6.2 us
  transfers between devices with their start and end apart: 12, of which 3 were waited for; matrix products, arithmetic and copies ran while one was open for 28% of the time, Pallas kernels for 0%

commit v1 on v0

--- a/solution.py
+++ b/solution.py
@@ -148,7 +148,12 @@
     bordered = extended(first_sweep, (("gx", 0), ("gz", 1)), 1)
     bordered = jnp.pad(bordered, ((0, 0), (0, 0), (1, 1)))
     pressure_next = relax_padded(bordered, pressure_pair[1], storage, source)
-    pressure_block = lax.all_to_all(pressure_next, "gz", split_axis=2, concat_axis=1, tiled=True)
+    pressure_block = jnp.concatenate(
+        lax.all_to_all(
+            jnp.stack(jnp.split(pressure_next, lax.axis_size("gz"), axis=2)), "gz", 0, 0
+        ),
+        axis=1,
+    )
     col_x, col_y, col_z = corner_terms(stress_next, pressure_block)
     node_main, node_rim = node_parts(col_x, col_y, col_z)
     from_below = passed_along(node_rim, "gz", 1)

time: 120 us -> 120 us (level)
    unnamed x38 -> x42, local copies, waits for them, and re-layouts: 2.45 us -> 3.23 us
where the time goes in v1:
time: 120 us; the launch traced here: 118 us
  other arithmetic  48.5 us (40%)
  starting transfers between devices  33.6 us (28%)
  local copies, waits for them, and re-layouts  20 us (17%)
  waiting for transfers between devices  15.3 us (13%)
    another operation x2, other arithmetic, on_device(): jnp.stack([pressure, conduct])  13.2 us
    ppermute x4, starting transfers between devices, extended(): after = lax.ppermute(leading, axis, down)  12.7 us
    ppermute x2, waiting for transfers between devices, passed_along(): return lax.ppermute(block, axis, route)  11.9 us
    max x1, other arithmetic, plastic(): jnp.maximum(1.0 - SHEAR * multiplier / jnp.maximum(equiv_shear, FLOOR), 0.0)  11.6 us
    div x1, other arithmetic, plastic(): return deviator * shrink_factor + normal_mask * (new_invariant / 3.0)  11.3 us
    scatter-add x1, local copies, waits for them, and re-layouts, on_device(): node_main = node_main.at[:, :, :, 0].add(from_below)  7.48 us
    ppermute x4, starting transfers between devices, extended(): before = lax.ppermute(last, axis, up)  7.03 us
    all_to_all x1, starting transfers between devices, on_device(): lax.all_to_all(jnp.stack(jnp.split(pressure_next, lax.axis_size('gz'), ax...  6.07 us
  transfers between devices with their start and end apart: 12, of which 3 were waited for; matrix products, arithmetic and copies ran while one was open for 28% of the time, Pallas kernels for 0%

profile of v1, /device:TPU:10, one launch (start us, length us, event | category | flops | bytes accessed | tf_op | source)
XLA Modules:
  0.0 118.5 jit_solution(4508041559652973038)
XLA Ops:
  0.6 2.0 %fusion.46 = (f32[1]{0:T(128)}, f32[1]{0:T(128)}, f32[1]{0:T(128)}, f32[1]{0:T(128)}, f32[1]{0:T(128)}, /*index=5*/f32[1]{0:T(128)}, f32[1]{0:T(128)}, f32[1]{0:...) fusion(f32[16]{0:T(128)} %param.23), kind=kLoop, calls=%fused_computation.151 | loop fusion | bytes 128 | tf_op jit(solution)/shard_map/slice | solution.py:35
  2.6 11.4 %add_bitcast_fusion = f32[1,2,128,256]{3,2,1,0:T(8,128)S(1)} fusion(s32[2,128,256]{2,1,0:T(8,128)} %param.22, f32[]{:T(128)} %bitcast.19, f32[]{:T(128)} %bitcast.18, f32[]{:T(128)} %bitcast.17, f32[]{:T(128)} %bitcast.16, f32[]{:T(128)} %bitcast.15, f32[]{:T(128)} %bitcast.14, f32[]{:T(128)} %bitcast.13, f32[]{:T(128)} %bitcast.12, f32[]{:T(128)} %bitcast.11, ...), kind=kLoop, calls=%fused_computation.126 | loop fusion | flops 3080192 | bytes 524352 | tf_op jit(solution)/shard_map/stack | solution.py:145
  14.0 0.7 copy-done.1
  14.7 1.8 %fusion.11 = (f32[2,1,128,256]{3,2,1,0:T(8,128)}, f32[2,1,128,256]{3,2,1,0:T(8,128)}) fusion(f32[1,2,128,256]{3,2,1,0:T(8,128)} %bitcast.81, f32[1,2,128,256]{3,2,1,0:T(8,128)S(1)} %add_bitcast_fusion), kind=kLoop, calls=%fused_computation.57 | loop fusion | flops 131072 | bytes 1048576 | tf_op jit(solution)/shard_map/stack | solution.py:145
  16.5 2.0 %collective-permute-start = (f32[2,1,128,256]{3,2,1,0:T(8,128)}, f32[2,1,128,256]{3,2,1,0:T(8,128)}, u32[]{:S(2)}, u32[]{:S(2)}) collective-permute-start(f32[2,1,128,256]{3,2,1,0:T(8,128)} %get-tuple-element.81), channel_id=1, source_target_pairs={{0,2},{2,4},{4,6},{6,8},{8,10},{10,12},{12,14},{14,16},{16,18},{18... | collective-permute-start | bytes 786440 | tf_op jit(solution)/shard_map/ppermute | solution.py:20
  18.5 4.5 %collective-permute-start.1 = (f32[2,1,128,256]{3,2,1,0:T(8,128)}, f32[2,1,128,256]{3,2,1,0:T(8,128)}, u32[]{:S(2)}, u32[]{:S(2)}) collective-permute-start(f32[2,1,128,256]{3,2,1,0:T(8,128)} %get-tuple-element.82), channel_id=1, source_target_pairs={{2,0},{4,2},{6,4},{8,6},{10,8},{12,10},{14,12},{16,14},{18,16},{20... | collective-permute-start | bytes 786440 | tf_op jit(solution)/shard_map/ppermute | solution.py:21
  23.2 0.9 copy.157
  24.1 4.6 %all-to-all-start = ((f32[2,256,128]{2,0,1:T(2,128)}), f32[2,256,128]{2,0,1:T(2,128)}, u32[]{:S(2)}, u32[]{:S(2)}) async-start(f32[2,256,128]{2,0,1:T(2,128)} %copy.157), calls=%async_computation | async-start | bytes 524288 | tf_op jit(solution)/shard_map/all_to_all | solution.py:141
  28.7 1.8 %multiply_add_fusion.1 = f32[6,2,256,128]{3,2,1,0:T(8,128)S(1)} fusion(f32[6,2,256,128]{3,2,1,0:T(8,128)} %param.16, f32[6,2,256,128]{3,2,1,0:T(8,128)S(1)} %copy-done.3, f32[2,256,128]{2,1,0:T(8,128)S(1)} %multiply_bitcast_fusion.1, f32[2,256,128]{2,1,0:T(8,128)S(1)} %get-tuple-element.59, f32[6]{0:T(128)S(1)} %copy-done.20), kind=kLoop, calls=%fused_computation.11 | loop fusion | flops 2359296 | bytes 5242904 | tf_op jit(solution)/shard_map/add | solution.py:68
  30.5 0.8 multiply_bitcast_fusion
  31.3 0.2 multiply_subtract_fusion.1
  31.5 0.5 copy-done.4
  32.0 0.3 copy-done
  32.4 0.8 pad_maximum_fusion.16
  33.2 1.3 %collective-permute-start.2 = (f32[2,4,1,256]{3,2,1,0:T(1,128)S(1)}, f32[2,4,1,256]{3,2,1,0:T(1,128)S(1)}, u32[]{:S(2)}, u32[]{:S(2)}) collective-permute-start(f32[2,4,1,256]{3,2,1,0:T(1,128)S(1)} %get-tuple-element.77), channel_id=1, source_target_pairs={{0,1},{2,3},{4,5},{6,7},{8,9},{10,11},{12,13},{14,15},{16,17},{18,... | collective-permute-start | bytes 24584 | tf_op jit(solution)/shard_map/ppermute | solution.py:20
  34.5 4.5 %collective-permute-start.3 = (f32[2,4,1,256]{3,2,1,0:T(1,128)S(1)}, f32[2,4,1,256]{3,2,1,0:T(1,128)S(1)}, u32[]{:S(2)}, u32[]{:S(2)}) collective-permute-start(f32[2,4,1,256]{3,2,1,0:T(1,128)S(1)} %get-tuple-element.78), channel_id=1, source_target_pairs={{1,0},{3,2},{5,4},{7,6},{9,8},{11,10},{13,12},{15,14},{17,16},{19,... | collective-permute-start | bytes 24584 | tf_op jit(solution)/shard_map/ppermute | solution.py:21
  39.1 1.1 broadcast_multiply_fusion
  40.1 0.9 copy.158
  41.0 1.9 %mul.293 = f32[2,128,256]{2,1,0:T(8,128)} reshape(f32[2,128,2,128]{3,2,1,0:T(2,128)} %copy.158) | data formatting | bytes 524288 | tf_op jit(solution)/shard_map/mul | solution.py:144
  42.9 1.7 %select_maximum_fusion = f32[2,4,130,258]{3,2,1,0:T(8,128)S(1)} fusion(f32[2,4,1,256]{3,2,1,0:T(1,128)S(1)} %collective-permute-done.3, f32[2,4,1,256]{3,2,1,0:T(1,128)S(1)} %collective-permute-done.2, f32[2,1,128,256]{3,2,1,0:T(8,128)} %collective-permute-done.1, f32[2,1,128,256]{3,2,1,0:T(8,128)} %collective-permute-done, f32[1,2,128,256]{3,2,1,0:T(8,128)} %copy-done.1, ...), kind=kLoop, calls=%fused_computation.2 | loop fusion | flops 3756480 | bytes 2138240 | tf_op jit(solution)/shard_map/concatenate | solution.py:22
  44.8 0.8 copy-done.8
  45.7 0.9 fusion.32
  46.6 1.9 %collective-permute-start.4 = (f32[1,128,256]{2,1,0:T(8,128)S(1)}, f32[1,128,256]{2,1,0:T(8,128)S(1)}, u32[]{:S(2)}, u32[]{:S(2)}) collective-permute-start(f32[1,128,256]{2,1,0:T(8,128)S(1)} %get-tuple-element.86), channel_id=1, source_target_pairs={{2,0},{4,2},{6,4},{8,6},{10,8},{12,10},{14,12},{16,14},{18,16},{20... | collective-permute-start | bytes 393224 | tf_op jit(solution)/shard_map/ppermute | solution.py:21
  48.5 2.4 %collective-permute-start.5 = (f32[1,128,256]{2,1,0:T(8,128)S(1)}, f32[1,128,256]{2,1,0:T(8,128)S(1)}, u32[]{:S(2)}, u32[]{:S(2)}) collective-permute-start(f32[1,128,256]{2,1,0:T(8,128)S(1)} %get-tuple-element.85), channel_id=1, source_target_pairs={{0,2},{2,4},{4,6},{6,8},{8,10},{10,12},{12,14},{14,16},{16,18},{18... | collective-permute-start | bytes 393224 | tf_op jit(solution)/shard_map/ppermute | solution.py:20
  51.0 0.7 fusion.44
  51.6 0.7 fusion.45
  52.3 3.4 %collective-permute-done.5 = f32[1,128,256]{2,1,0:T(8,128)S(1)} collective-permute-done((f32[1,128,256]{2,1,0:T(8,128)S(1)}, f32[1,128,256]{2,1,0:T(8,128)S(1)}, u32[]{:S(2)}, u32[]{:S(2)}) %collective-permute-start.5) | collective-permute-done | bytes 131104 | tf_op jit(solution)/shard_map/ppermute | solution.py:20
  55.7 1.7 %collective-permute-start.6 = (f32[4,1,256]{2,1,0:T(1,128)S(1)}, f32[4,1,256]{2,1,0:T(1,128)S(1)}, u32[]{:S(2)}, u32[]{:S(2)}) collective-permute-start(f32[4,1,256]{2,1,0:T(1,128)S(1)} %get-tuple-element.80), channel_id=1, source_target_pairs={{1,0},{3,2},{5,4},{7,6},{9,8},{11,10},{13,12},{15,14},{17,16},{19,... | collective-permute-start | bytes 12296 | tf_op jit(solution)/shard_map/ppermute | solution.py:21
  57.4 1.3 %collective-permute-start.7 = (f32[4,1,256]{2,1,0:T(1,128)S(1)}, f32[4,1,256]{2,1,0:T(1,128)S(1)}, u32[]{:S(2)}, u32[]{:S(2)}) collective-permute-start(f32[4,1,256]{2,1,0:T(1,128)S(1)} %get-tuple-element.79), channel_id=1, source_target_pairs={{0,1},{2,3},{4,5},{6,7},{8,9},{10,11},{12,13},{14,15},{16,17},{18,... | collective-permute-start | bytes 12296 | tf_op jit(solution)/shard_map/ppermute | solution.py:20
  58.7 11.6 %subtract_maximum_fusion = (f32[2,256,128]{2,1,0:T(8,128)}, f32[2,256,128]{2,1,0:T(8,128)}, pred[2,256,128]{2,1,0:T(8,128)(4,1)S(1)}, pred[2,256,128]{2,1,0:T(8,...) fusion(f32[]{:T(128)} %bitcast.43, f32[]{:T(128)} %bitcast.42, ...), kind=kLoop, calls=%fused_computation.115 | loop fusion | flops 4063232 | bytes 3145792 | tf_op jit(solution)/shard_map/max | solution.py:88
  70.3 0.3 select_maximum_fusion.5
  70.6 0.8 fusion.21
  71.4 0.7 copy-done.12
  72.2 0.7 pad_maximum_fusion.12
  72.9 6.1 %all-to-all-start.1 = ((f32[2,2,128,128]{3,2,1,0:T(8,128)}), f32[2,2,128,128]{3,2,1,0:T(8,128)S(1)}, u32[]{:S(2)}, u32[]{:S(2)}) async-start(f32[2,2,128,128]{3,2,1,0:T(8,128)} %pad_maximum_fusion.12), calls=%async_computation.1 | async-start | bytes 524288 | tf_op jit(solution)/shard_map/all_to_all | solution.py:152
  79.0 11.3 %fusion.10 = f32[2,256,128]{2,1,0:T(8,128)S(1)} fusion(f32[1,2,256,128]{3,2,1,0:T(8,128)S(1)} %copy-done.7, pred[2,256,128]{2,1,0:T(8,128)(4,1)} %get-tuple-element.56, f32[]{:T(128)} %bitcast.43, pred[2,256,128]{2,1,0:T(8,128)(4,1)} %get-tuple-element.55, f32[]{:T(128)} %bitcast.42, pred[2,256,128]{2,1,0:T(8,128)(4,1)S(1)} %copy-done.17, f32[]{:T(128)} %bitcast.41, ...), kind=kLoop, calls=%fused_computation.56 | loop fusion | flops 2686976 | bytes 1310784 | tf_op jit(solution)/shard_map/div | solution.py:90
  90.4 1.6 %multiply_subtract_fusion = (f32[6,2,256,128]{3,2,1,0:T(8,128)S(1)}, f32[6,2,256,128]{3,2,1,0:T(8,128)}) fusion(f32[2,256,128]{2,1,0:T(8,128)S(1)} %bitcast.85, f32[6]{0:T(128)S(1)} %copy-done.20, f32[2,256,128]{2,1,0:T(8,128)S(1)} %fusion.10, f32[2,256,128]{2,1,0:T(8,128)S(1)} %copy-done.9, f32[6,2,256,128]{3,2,1,0:T(8,128)S(1)} %multiply_add_fusion.1, ...), kind=kLoop, calls=%fused_computation.8 | loop fusion | flops 2752512 | bytes 5767192 | tf_op jit(solution)/shard_map/sub | solution.py:95
  92.4 0.2 add_multiply_fusion
  92.6 0.2 add_multiply_fusion.4
  93.1 0.7 slice_reduce_fusion
  93.8 1.3 %collective-permute-start.8 = (f32[3,3,256]{2,1,0:T(4,128)S(1)}, f32[3,3,256]{2,1,0:T(4,128)S(1)}, u32[]{:S(2)}, u32[]{:S(2)}) collective-permute-start(f32[3,3,256]{2,1,0:T(4,128)S(1)} %slice_reduce_fusion), channel_id=1, source_target_pairs={{0,1},{2,3},{4,5},{6,7},{8,9},{10,11},{12,13},{14,15},{16,17},{18,... | collective-permute-start | bytes 27656 | tf_op jit(solution)/shard_map/ppermute | solution.py:29
  95.1 0.5 fusion.3
  95.6 3.8 %collective-permute-done.8 = f32[3,3,256]{2,1,0:T(4,128)S(1)} collective-permute-done((f32[3,3,256]{2,1,0:T(4,128)S(1)}, f32[3,3,256]{2,1,0:T(4,128)S(1)}, u32[]{:S(2)}, u32[]{:S(2)}) %collective-permute-start.8) | collective-permute-done | bytes 9248 | tf_op jit(solution)/shard_map/ppermute | solution.py:29
  99.4 0.4 copy.160
  99.9 7.5 %scatter-add.6 = f32[3,3,256,128]{3,2,1,0:T(8,128)S(1)} dynamic-update-slice(f32[3,3,256,128]{3,2,1,0:T(8,128)S(1)} %fusion.3, f32[3,3,256,1]{3,2,1,0:T(8,128)S(1)} %slice_add_fusion, s32[]{:T(128)} %constant.100.clone.1, s32[]{:T(128)} %constant.100.clone.1, s32[]{:T(128)} %constant.100.clone.1, s32[]{:T(128)} %constant.100.clone.1) | dynamic-update-slice | bytes 18436 | tf_op jit(solution)/shard_map/scatter-add | solution.py:160
  107.4 1.9 %collective-permute-start.9 = (f32[3,256,128]{2,1,0:T(8,128)S(1)}, f32[3,256,128]{2,1,0:T(8,128)S(1)}, u32[]{:S(2)}, u32[]{:S(2)}) collective-permute-start(f32[3,256,128]{2,1,0:T(8,128)S(1)} %slice_bitcast_fusion.2), channel_id=1, source_target_pairs={{0,2},{2,4},{4,6},{6,8},{8,10},{10,12},{12,14},{14,16},{16,18},{18... | collective-permute-start | bytes 1179656 | tf_op jit(solution)/shard_map/ppermute | solution.py:29
  109.4 8.1 %collective-permute-done.9 = f32[3,256,128]{2,1,0:T(8,128)S(1)} collective-permute-done((f32[3,256,128]{2,1,0:T(8,128)S(1)}, f32[3,256,128]{2,1,0:T(8,128)S(1)}, u32[]{:S(2)}, u32[]{:S(2)}) %collective-permute-start.9) | collective-permute-done | bytes 393248 | tf_op jit(solution)/shard_map/ppermute | solution.py:29
  117.5 0.9 slice.475
  (60 shorter events, 1.4 us)
Async XLA Ops:
  0.6 22.5 %copy-start.3 = (f32[6,2,256,128]{3,2,1,0:T(8,128)S(1)}, f32[6,2,256,128]{3,2,1,0:T(8,128)}, u32[]{:S(2)}) copy-start(f32[6,2,256,128]{3,2,1,0:T(8,128)} %param.15) | copy-start | bytes 4718596
  14.0 0.7 copy-start.1
  16.5 12.2 %copy-start.20 = (f32[6]{0:T(128)S(1)}, f32[6]{0:T(128)}, u32[]{:S(2)}) copy-start(f32[6]{0:T(128)} %constant.126.clone) | copy-start | bytes 76
  16.5 15.5 %collective-permute-start = (f32[2,1,128,256]{3,2,1,0:T(8,128)}, f32[2,1,128,256]{3,2,1,0:T(8,128)}, u32[]{:S(2)}, u32[]{:S(2)}) collective-permute-start(f32[2,1,128,256]{3,2,1,0:T(8,128)} %get-tuple-element.81), channel_id=1, source_target_pairs={{0,2},{2,4},{4,6},{6,8},{8,10},{10,12},{12,14},{14,16},{16,18},{18... | collective-permute-start | bytes 786440 | tf_op jit(solution)/shard_map/ppermute | solution.py:20
  18.5 13.4 %collective-permute-start.1 = (f32[2,1,128,256]{3,2,1,0:T(8,128)}, f32[2,1,128,256]{3,2,1,0:T(8,128)}, u32[]{:S(2)}, u32[]{:S(2)}) collective-permute-start(f32[2,1,128,256]{3,2,1,0:T(8,128)} %get-tuple-element.82), channel_id=1, source_target_pairs={{2,0},{4,2},{6,4},{8,6},{10,8},{12,10},{14,12},{16,14},{18,16},{20... | collective-permute-start | bytes 786440 | tf_op jit(solution)/shard_map/ppermute | solution.py:21
  24.1 15.0 %all-to-all-start = ((f32[2,256,128]{2,0,1:T(2,128)}), f32[2,256,128]{2,0,1:T(2,128)}, u32[]{:S(2)}, u32[]{:S(2)}) async-start(f32[2,256,128]{2,0,1:T(2,128)} %copy.157), calls=%async_computation | async-start | bytes 524288 | tf_op jit(solution)/shard_map/all_to_all | solution.py:141
  31.3 0.7 copy-start.4
  31.3 1.0 copy-start
  31.3 1.1 copy-start.2
  33.2 9.7 %collective-permute-start.2 = (f32[2,4,1,256]{3,2,1,0:T(1,128)S(1)}, f32[2,4,1,256]{3,2,1,0:T(1,128)S(1)}, u32[]{:S(2)}, u32[]{:S(2)}) collective-permute-start(f32[2,4,1,256]{3,2,1,0:T(1,128)S(1)} %get-tuple-element.77), channel_id=1, source_target_pairs={{0,1},{2,3},{4,5},{6,7},{8,9},{10,11},{12,13},{14,15},{16,17},{18,... | collective-permute-start | bytes 24584 | tf_op jit(solution)/shard_map/ppermute | solution.py:20
  34.5 8.4 %collective-permute-start.3 = (f32[2,4,1,256]{3,2,1,0:T(1,128)S(1)}, f32[2,4,1,256]{3,2,1,0:T(1,128)S(1)}, u32[]{:S(2)}, u32[]{:S(2)}) collective-permute-start(f32[2,4,1,256]{3,2,1,0:T(1,128)S(1)} %get-tuple-element.78), channel_id=1, source_target_pairs={{1,0},{3,2},{5,4},{7,6},{9,8},{11,10},{13,12},{15,14},{17,16},{19,... | collective-permute-start | bytes 24584 | tf_op jit(solution)/shard_map/ppermute | solution.py:21
  44.6 1.0 copy-start.8
  44.6 1.0 copy-start.11
  45.7 5.3 %copy-start.18 = (f32[8]{0:T(128)S(1)}, f32[8]{0:T(128)}, u32[]{:S(2)}) copy-start(f32[8]{0:T(128)} %param.19) | copy-start | bytes 100
  45.7 6.0 %copy-start.19 = (f32[8]{0:T(128)S(1)}, f32[8]{0:T(128)}, u32[]{:S(2)}) copy-start(f32[8]{0:T(128)} %param.18) | copy-start | bytes 100
  45.7 13.1 %copy-start.6 = (f32[1,2,256,128]{3,2,1,0:T(8,128)S(1)}, f32[1,2,256,128]{3,2,1,0:T(8,128)}, u32[]{:S(2)}) copy-start(f32[1,2,256,128]{3,2,1,0:T(8,128)} %get-tuple-element.58) | copy-start | bytes 786436
  45.7 13.1 %copy-start.13 = (s32[2,256,128]{2,1,0:T(8,128)S(1)}, s32[2,256,128]{2,1,0:T(8,128)}, u32[]{:S(2)}) copy-start(s32[2,256,128]{2,1,0:T(8,128)} %param.17) | copy-start | bytes 786436
  46.6 5.7 %collective-permute-start.4 = (f32[1,128,256]{2,1,0:T(8,128)S(1)}, f32[1,128,256]{2,1,0:T(8,128)S(1)}, u32[]{:S(2)}, u32[]{:S(2)}) collective-permute-start(f32[1,128,256]{2,1,0:T(8,128)S(1)} %get-tuple-element.86), channel_id=1, source_target_pairs={{2,0},{4,2},{6,4},{8,6},{10,8},{12,10},{14,12},{16,14},{18,16},{20... | collective-permute-start | bytes 393224 | tf_op jit(solution)/shard_map/ppermute | solution.py:21
  48.5 7.2 %collective-permute-start.5 = (f32[1,128,256]{2,1,0:T(8,128)S(1)}, f32[1,128,256]{2,1,0:T(8,128)S(1)}, u32[]{:S(2)}, u32[]{:S(2)}) collective-permute-start(f32[1,128,256]{2,1,0:T(8,128)S(1)} %get-tuple-element.85), channel_id=1, source_target_pairs={{0,2},{2,4},{4,6},{6,8},{8,10},{10,12},{12,14},{14,16},{16,18},{18... | collective-permute-start | bytes 393224 | tf_op jit(solution)/shard_map/ppermute | solution.py:20
  55.7 14.6 %collective-permute-start.6 = (f32[4,1,256]{2,1,0:T(1,128)S(1)}, f32[4,1,256]{2,1,0:T(1,128)S(1)}, u32[]{:S(2)}, u32[]{:S(2)}) collective-permute-start(f32[4,1,256]{2,1,0:T(1,128)S(1)} %get-tuple-element.80), channel_id=1, source_target_pairs={{1,0},{3,2},{5,4},{7,6},{9,8},{11,10},{13,12},{15,14},{17,16},{19,... | collective-permute-start | bytes 12296 | tf_op jit(solution)/shard_map/ppermute | solution.py:21
  57.4 12.9 %collective-permute-start.7 = (f32[4,1,256]{2,1,0:T(1,128)S(1)}, f32[4,1,256]{2,1,0:T(1,128)S(1)}, u32[]{:S(2)}, u32[]{:S(2)}) collective-permute-start(f32[4,1,256]{2,1,0:T(1,128)S(1)} %get-tuple-element.79), channel_id=1, source_target_pairs={{0,1},{2,3},{4,5},{6,7},{8,9},{10,11},{12,13},{14,15},{16,17},{18,... | collective-permute-start | bytes 12296 | tf_op jit(solution)/shard_map/ppermute | solution.py:20
  71.4 0.7 copy-start.12
  72.1 6.9 %copy-start.7 = (f32[1,2,256,128]{3,2,1,0:T(8,128)S(1)}, f32[1,2,256,128]{3,2,1,0:T(8,128)}, u32[]{:S(2)}) copy-start(f32[1,2,256,128]{3,2,1,0:T(8,128)} %get-tuple-element.58) | copy-start | bytes 786436
  72.1 6.9 %copy-start.10 = (f32[2,256,128]{2,1,0:T(8,128)S(1)}, f32[2,256,128]{2,1,0:T(8,128)}, u32[]{:S(2)}) copy-start(f32[2,256,128]{2,1,0:T(8,128)} %get-tuple-element.48) | copy-start | bytes 786436
  72.1 6.9 %copy-start.14 = (pred[2,256,128]{2,1,0:T(8,128)(4,1)S(1)}, pred[2,256,128]{2,1,0:T(8,128)(4,1)}, u32[]{:S(2)}) copy-start(pred[2,256,128]{2,1,0:T(8,128)(4,1)} %get-tuple-element.51) | copy-start | bytes 196612
  72.1 6.9 %copy-start.15 = (pred[2,256,128]{2,1,0:T(8,128)(4,1)S(1)}, pred[2,256,128]{2,1,0:T(8,128)(4,1)}, u32[]{:S(2)}) copy-start(pred[2,256,128]{2,1,0:T(8,128)(4,1)} %get-tuple-element.52) | copy-start | bytes 196612
  72.2 6.9 %copy-start.16 = (pred[2,256,128]{2,1,0:T(8,128)(4,1)S(1)}, pred[2,256,128]{2,1,0:T(8,128)(4,1)}, u32[]{:S(2)}) copy-start(pred[2,256,128]{2,1,0:T(8,128)(4,1)} %get-tuple-element.53) | copy-start | bytes 196612
  72.2 6.9 %copy-start.17 = (pred[2,256,128]{2,1,0:T(8,128)(4,1)S(1)}, pred[2,256,128]{2,1,0:T(8,128)(4,1)}, u32[]{:S(2)}) copy-start(pred[2,256,128]{2,1,0:T(8,128)(4,1)} %get-tuple-element.54) | copy-start | bytes 196612
  72.2 18.1 %copy-start.5 = (f32[2,256,128]{2,1,0:T(8,128)S(1)}, f32[2,256,128]{2,1,0:T(8,128)}, u32[]{:S(2)}) copy-start(f32[2,256,128]{2,1,0:T(8,128)} %copy-done.4) | copy-start | bytes 786436
  72.2 18.1 %copy-start.9 = (f32[2,256,128]{2,1,0:T(8,128)S(1)}, f32[2,256,128]{2,1,0:T(8,128)}, u32[]{:S(2)}) copy-start(f32[2,256,128]{2,1,0:T(8,128)} %get-tuple-element.47) | copy-start | bytes 786436
  72.9 17.4 %all-to-all-start.1 = ((f32[2,2,128,128]{3,2,1,0:T(8,128)}), f32[2,2,128,128]{3,2,1,0:T(8,128)S(1)}, u32[]{:S(2)}, u32[]{:S(2)}) async-start(f32[2,2,128,128]{3,2,1,0:T(8,128)} %pad_maximum_fusion.12), calls=%async_computation.1 | async-start | bytes 524288 | tf_op jit(solution)/shard_map/all_to_all | solution.py:152
  93.8 5.6 %collective-permute-start.8 = (f32[3,3,256]{2,1,0:T(4,128)S(1)}, f32[3,3,256]{2,1,0:T(4,128)S(1)}, u32[]{:S(2)}, u32[]{:S(2)}) collective-permute-start(f32[3,3,256]{2,1,0:T(4,128)S(1)} %slice_reduce_fusion), channel_id=1, source_target_pairs={{0,1},{2,3},{4,5},{6,7},{8,9},{10,11},{12,13},{14,15},{16,17},{18,... | collective-permute-start | bytes 27656 | tf_op jit(solution)/shard_map/ppermute | solution.py:29
  107.4 10.0 %collective-permute-start.9 = (f32[3,256,128]{2,1,0:T(8,128)S(1)}, f32[3,256,128]{2,1,0:T(8,128)S(1)}, u32[]{:S(2)}, u32[]{:S(2)}) collective-permute-start(f32[3,256,128]{2,1,0:T(8,128)S(1)} %slice_bitcast_fusion.2), channel_id=1, source_target_pairs={{0,2},{2,4},{4,6},{6,8},{8,10},{10,12},{12,14},{14,16},{16,18},{18... | collective-permute-start | bytes 1179656 | tf_op jit(solution)/shard_map/ppermute | solution.py:29
